TPU v7x, 512 devices: a whole 4x4x16 slice. The times are simulated.
512 devices in a mesh: req: 4 (over x), head: 8 (over y, core), ctx: 16 (over z).
Axes of the slice: x: 4, y: 4, z: 16, core: 2. Of those that a mesh axis runs over, the one named last changes fastest.
Arguments:
- queries: bfloat16 [32768, 2048], P(('req', 'ctx'), 'head'), parts along dimension 0, may hold values from -8 to 8
- keys_own: bfloat16 [32768, 2048], P(('req', 'ctx'), 'head'), parts along dimension 0, may hold values from -8 to 8
- values_own: bfloat16 [32768, 2048], P(('req', 'ctx'), 'head'), parts along dimension 0, may hold values from -6 to 6
- keys_cache: bfloat16 [262144, 2048], P(('req', 'ctx'), 'head'), parts along dimension 0, may hold values from -8 to 8
- values_cache: bfloat16 [262144, 2048], P(('req', 'ctx'), 'head'), parts along dimension 0, may hold values from -6 to 6
- picks: int32 [64, 16, 3], P(('req', 'ctx'), 'head'), parts along dimension 0, may hold values from 0 to 15, as said below
Outputs:
- attended: bfloat16 [32768, 2048], P(('req', 'ctx'), 'head'), parts along dimension 0
There are 4 independent parts, one for each index of `req`. A program takes and returns all parts, laid end to end along the dimension named above; each array names one. Nothing has to cross between parts.
Inputs may be any that keep to these rules, and one draw needn't show every extreme that they name: Block b is stored on ctx index b. The 3 picks of one tile and head name blocks on different ctx indices. Among the picks of one tile over the 2 heads of one head index, at most 1 name blocks on any one ctx index, and exactly 1 do for a ctx index that is the same for all tiles.
All inputs are finite; a program needn't handle non-finite values.
Results may differ from a plain program's by a relative error of at most 0.0048.
Values may be sent and summed in bfloat16 or wider, within the bound.
A program may use at most 64 MiB of HBM per device.

v0:
```python
import jax
import jax.numpy as jnp
from jax import lax
from jax.sharding import PartitionSpec as P

BLOCK = 4096
BLK_DEV = 1


NEG = -1e30


def attend(query, keys, values, bias):
    scores = (
        lax.dot_general(query, keys, (((1,), (1,)), ((), ())), preferred_element_type=jnp.float32)
        * query.shape[-1] ** (-0.5)
        + bias
    )
    top = jnp.max(scores, axis=-1)
    expo = jnp.exp(scores - top[:, None])
    total = jnp.sum(expo, axis=-1)
    summed = jnp.dot(expo.astype(jnp.bfloat16), values, preferred_element_type=jnp.float32)
    return (summed, top, total)


def combine(summed, top, total):
    best = jnp.max(top, axis=0)
    factor = jnp.exp(top - best[None])
    numer = jnp.sum(summed * factor[..., None], axis=0)
    denom = jnp.sum(total * factor, axis=0)
    return (numer / denom[..., None]).astype(jnp.bfloat16)


def shards(queries, keys_own, values_own, keys_cache, values_cache, picks):
    owners = lax.axis_size("ctx")
    heads_dev = picks.shape[1]
    top_count = picks.shape[2]
    tile_rows = queries.shape[0]
    head_dim = queries.shape[1] // heads_dev
    pick_count = heads_dev * top_count
    slot_cap = (pick_count + owners - 1) // owners
    slot_count = owners * slot_cap
    query_heads = queries.reshape(tile_rows, heads_dev, head_dim).transpose(1, 0, 2)
    key_heads = keys_own.reshape(tile_rows, heads_dev, head_dim).transpose(1, 0, 2)
    value_heads = values_own.reshape(tile_rows, heads_dev, head_dim).transpose(1, 0, 2)
    flat_picks = picks.reshape(pick_count)
    owner_of = flat_picks // BLK_DEV
    local_block = flat_picks % BLK_DEV
    head_of = jnp.arange(pick_count, dtype=jnp.int32) // top_count
    owner_hit = (owner_of[:, None] == jnp.arange(owners, dtype=jnp.int32)[None, :]).astype(
        jnp.int32
    )
    slot_rank = jnp.sum((jnp.cumsum(owner_hit, axis=0) - owner_hit) * owner_hit, axis=1)
    slot_of = owner_of * slot_cap + slot_rank
    placed = slot_of[None, :] == jnp.arange(slot_count, dtype=jnp.int32)[:, None]
    occupied = jnp.any(placed, axis=1)
    slot_head = jnp.sum(jnp.where(placed, head_of[None, :], 0), axis=1)
    slot_block = jnp.sum(jnp.where(placed, local_block[None, :], 0), axis=1)
    marked_head = jnp.where(occupied, slot_head, -1)
    request_table = jnp.stack([marked_head, slot_block], axis=1).reshape(owners, slot_cap, 2)
    cache_keys = keys_cache.reshape(BLK_DEV, BLOCK, heads_dev, head_dim)
    cache_values = values_cache.reshape(BLK_DEV, BLOCK, heads_dev, head_dim)
    zero_bias = jnp.zeros((), jnp.float32)

    def answer(query, request):

        def compute(unused):
            head = jnp.maximum(request[0], 0)
            return attend(
                query, cache_keys[request[1], :, head], cache_values[request[1], :, head], zero_bias
            )

        def skipped(unused):
            return (
                jnp.zeros((tile_rows, head_dim), jnp.float32),
                jnp.zeros((tile_rows,), jnp.float32),
                jnp.zeros((tile_rows,), jnp.float32),
            )

        return lax.cond(request[0] >= 0, compute, skipped, 0)

    position = jnp.arange(tile_rows)
    causal = jnp.where(position[:, None] >= position[None, :], 0.0, NEG).astype(jnp.float32)
    summed, top, total = jax.vmap(attend, in_axes=(0, 0, 0, None))(
        query_heads, key_heads, value_heads, causal
    )
    own = (summed[None], top[None], total[None])
    request_in = lax.all_to_all(request_table, "ctx", split_axis=0, concat_axis=0, tiled=True)
    gathered = lax.all_gather(queries, "ctx", axis=0, tiled=True).reshape(
        owners, tile_rows, heads_dev, head_dim
    )
    source_of = jnp.arange(slot_count, dtype=jnp.int32) // slot_cap

    def answer_tile(pieces):
        source, request = pieces
        query = gathered[source, :, jnp.maximum(request[0], 0)]
        return answer(query, request)

    summed_in, top_in, total_in = lax.map(answer_tile, (source_of, request_in.reshape(-1, 2)))
    summed = lax.all_to_all(
        summed_in.reshape(owners, slot_cap, tile_rows, head_dim),
        "ctx",
        split_axis=0,
        concat_axis=0,
        tiled=True,
    )
    top = lax.all_to_all(
        top_in.reshape(owners, slot_cap, tile_rows), "ctx", split_axis=0, concat_axis=0, tiled=True
    )
    total = lax.all_to_all(
        total_in.reshape(owners, slot_cap, tile_rows),
        "ctx",
        split_axis=0,
        concat_axis=0,
        tiled=True,
    )
    summed = summed.reshape(slot_count, tile_rows, head_dim)[slot_of]
    top = top.reshape(slot_count, tile_rows)[slot_of]
    total = total.reshape(slot_count, tile_rows)[slot_of]
    summed = summed.reshape(heads_dev, top_count, tile_rows, head_dim).transpose(1, 0, 2, 3)
    top = top.reshape(heads_dev, top_count, tile_rows).transpose(1, 0, 2)
    total = total.reshape(heads_dev, top_count, tile_rows).transpose(1, 0, 2)
    remote = (summed, top, total)
    summed = jnp.concatenate([own[0], remote[0]], axis=0)
    top = jnp.concatenate([own[1], remote[1]], axis=0)
    total = jnp.concatenate([own[2], remote[2]], axis=0)
    mixed = combine(summed, top, total)
    return mixed.transpose(1, 0, 2).reshape(tile_rows, heads_dev * head_dim)


def solution(mesh):
    placed = (
        P(("req", "ctx"), "head"),
        P(("req", "ctx"), "head"),
        P(("req", "ctx"), "head"),
        P(("req", "ctx"), "head"),
        P(("req", "ctx"), "head"),
        P(("req", "ctx"), "head", None),
    )
    return jax.shard_map(
        shards, mesh=mesh, in_specs=placed, out_specs=P(("req", "ctx"), "head"), check_vma=False
    )
```

profile of v0, /device:TPU:40, one launch (start us, length us, event | category | flops | bytes accessed | tf_op | source)
XLA Modules:
  0.0 516.6 jit_solution(1000211270126715552)
XLA Ops:
  7.3 0.8 reshape.170
  9.2 15.2 %all-to-all-start = ((s32[16,1,2]{2,1,0:T(1,128)}), s32[16,1,2]{2,1,0:T(1,128)S(1)}, u32[]{:S(2)}, u32[]{:S(2)}) async-start(s32[16,1,2]{2,1,0:T(1,128)} %copy.66), calls=%async_computation | async-start | bytes 16384 | tf_op jit(solution)/shard_map/all_to_all | solution.py:88
  24.4 2.9 copy.69
  27.4 2.5 copy.73
  29.9 4.1 copy.70
  34.0 3.1 copy.74
  37.1 55.0 %all-gather.2.cloned.1.call-done = bf16[8192,256]{1,0:T(8,128)(2,1)} async-done(((bf16[512,256]{1,0:T(8,128)(2,1)}), bf16[8192,256]{1,0:T(8,128)(2,1)}) %all-gather.2.cloned.1.call-update) | async-done | bytes 4194320 | tf_op jit(solution)/shard_map/all_gather | solution.py:89
  92.1 6.9 %reshape.211 = bf16[16,512,2,128]{3,2,1,0:T(2,128)(2,1)} reshape(bf16[8192,256]{1,0:T(8,128)(2,1)} %all-gather.2.cloned.1.call-done) | data formatting | bytes 8388608 | tf_op jit(solution)/shard_map/reshape | solution.py:89
  99.1 5.1 copy.72
  104.2 92.7 %while.15 = (s32[]{:T(128)}, f32[16,512,128]{2,1,0:T(8,128)}, f32[16,512]{1,0:T(8,128)S(1)}, f32[16,512]{1,0:T(8,128)S(1)}, s32[16,2]{1,0:T(8,128)S(1)}, /*index...) while((s32[]{:T(128)}, f32[16,512,128]{2,1,0:T(8,128)}, ...), condition=%wide.region_10.11_spmd.clone, body=%wide.region_5.10_spmd.clone.sunk | while | flops 1090518016 | bytes 28198256 | solution.py:99
  111.5 0.7 constant_dynamic-update-slice_fusion.2
  113.1 10.2 %conditional.3 = (f32[1,512,128]{2,1,0:T(8,128)S(1)}, f32[1,512]{1,0:T(1,128)}, f32[1,512]{1,0:T(1,128)S(1)}) conditional(s32[]{:T(128)} %convert_element_type.33, () %tuple.55, (s32[16]{0:T(128)S(1)}, s32[]{:T(128)}, s32[]{:T(128)S(1)}, bf16[16,512,2,128]{3,1,2,0:T(8,128)(2,1)}, s32[1,2]{1,0:T(1,128)S(1)}, ...), branch_computations={%region_6.6_spmd, %region_7.9_spmd} | conditional | flops 1090518016 | bytes 27665002 | solution.py:80
  115.7 3.2 multiply_reduce_fusion
  118.9 2.2 fusion.6
  121.1 2.2 fusion.2
  123.2 0.7 constant_dynamic-update-slice_fusion.2
  124.8 10.2 %conditional.3 = (f32[1,512,128]{2,1,0:T(8,128)S(1)}, f32[1,512]{1,0:T(1,128)}, f32[1,512]{1,0:T(1,128)S(1)}) conditional(s32[]{:T(128)} %convert_element_type.33, () %tuple.55, (s32[16]{0:T(128)S(1)}, s32[]{:T(128)}, s32[]{:T(128)S(1)}, bf16[16,512,2,128]{3,1,2,0:T(8,128)(2,1)}, s32[1,2]{1,0:T(1,128)S(1)}, ...), branch_computations={%region_6.6_spmd, %region_7.9_spmd} | conditional | flops 1090518016 | bytes 27665002 | solution.py:80
  127.5 3.2 multiply_reduce_fusion
  130.7 2.1 fusion.6
  132.8 2.2 fusion.2
  135.0 0.7 constant_dynamic-update-slice_fusion.2
  138.8 10.2 %conditional.3 = (f32[1,512,128]{2,1,0:T(8,128)S(1)}, f32[1,512]{1,0:T(1,128)}, f32[1,512]{1,0:T(1,128)S(1)}) conditional(s32[]{:T(128)} %convert_element_type.33, () %tuple.55, (s32[16]{0:T(128)S(1)}, s32[]{:T(128)}, s32[]{:T(128)S(1)}, bf16[16,512,2,128]{3,1,2,0:T(8,128)(2,1)}, s32[1,2]{1,0:T(1,128)S(1)}, ...), branch_computations={%region_6.6_spmd, %region_7.9_spmd} | conditional | flops 1090518016 | bytes 27665002 | solution.py:80
  141.5 3.2 multiply_reduce_fusion
  144.7 2.2 fusion.6
  146.8 2.2 fusion.2
  149.0 0.7 constant_dynamic-update-slice_fusion.2
  152.8 10.2 %conditional.3 = (f32[1,512,128]{2,1,0:T(8,128)S(1)}, f32[1,512]{1,0:T(1,128)}, f32[1,512]{1,0:T(1,128)S(1)}) conditional(s32[]{:T(128)} %convert_element_type.33, () %tuple.55, (s32[16]{0:T(128)S(1)}, s32[]{:T(128)}, s32[]{:T(128)S(1)}, bf16[16,512,2,128]{3,1,2,0:T(8,128)(2,1)}, s32[1,2]{1,0:T(1,128)S(1)}, ...), branch_computations={%region_6.6_spmd, %region_7.9_spmd} | conditional | flops 1090518016 | bytes 27665002 | solution.py:80
  155.4 3.2 multiply_reduce_fusion
  158.7 2.2 fusion.6
  160.8 2.2 fusion.2
  165.2 0.7 constant_dynamic-update-slice_fusion.2
  166.8 10.2 %conditional.3 = (f32[1,512,128]{2,1,0:T(8,128)S(1)}, f32[1,512]{1,0:T(1,128)}, f32[1,512]{1,0:T(1,128)S(1)}) conditional(s32[]{:T(128)} %convert_element_type.33, () %tuple.55, (s32[16]{0:T(128)S(1)}, s32[]{:T(128)}, s32[]{:T(128)S(1)}, bf16[16,512,2,128]{3,1,2,0:T(8,128)(2,1)}, s32[1,2]{1,0:T(1,128)S(1)}, ...), branch_computations={%region_6.6_spmd, %region_7.9_spmd} | conditional | flops 1090518016 | bytes 27665002 | solution.py:80
  169.4 3.2 multiply_reduce_fusion
  172.6 2.1 fusion.6
  174.8 2.2 fusion.2
  177.0 0.7 constant_dynamic-update-slice_fusion.2
  185.2 10.2 %conditional.3 = (f32[1,512,128]{2,1,0:T(8,128)S(1)}, f32[1,512]{1,0:T(1,128)}, f32[1,512]{1,0:T(1,128)S(1)}) conditional(s32[]{:T(128)} %convert_element_type.33, () %tuple.55, (s32[16]{0:T(128)S(1)}, s32[]{:T(128)}, s32[]{:T(128)S(1)}, bf16[16,512,2,128]{3,1,2,0:T(8,128)(2,1)}, s32[1,2]{1,0:T(1,128)S(1)}, ...), branch_computations={%region_6.6_spmd, %region_7.9_spmd} | conditional | flops 1090518016 | bytes 27665002 | solution.py:80
  187.8 3.2 multiply_reduce_fusion
  191.0 2.2 fusion.6
  193.2 2.2 fusion.2
  195.3 0.7 constant_dynamic-update-slice_fusion.2
  197.5 103.6 %all-to-all-start.2 = ((f32[16,1,512]{2,1,0:T(1,128)}), f32[16,1,512]{2,1,0:T(1,128)S(1)}, u32[]{:S(2)}, u32[]{:S(2)}) async-start(f32[16,1,512]{2,1,0:T(1,128)} %reshape.180), calls=%async_computation.2 | async-start | bytes 65536 | tf_op jit(solution)/shard_map/all_to_all | solution.py:107
  301.2 11.4 %all-to-all-done.2 = f32[16,1,512]{2,1,0:T(1,128)S(1)} async-done(((f32[16,1,512]{2,1,0:T(1,128)}), f32[16,1,512]{2,1,0:T(1,128)S(1)}, u32[]{:S(2)}, u32[]{:S(2)}) %all-to-all-start.2) | async-done | bytes 32800 | tf_op jit(solution)/shard_map/all_to_all | solution.py:107
  312.6 15.0 %all_to_all.20 = f32[16,1,512]{2,1,0:T(1,128)S(1)} all-to-all(f32[16,1,512]{2,1,0:T(1,128)S(1)} %reshape.183), channel_id=1, replica_groups=mesh['req'=4,'head'=8,'ctx'=16] {'ctx'}, dimensions={0} | all-to-all | bytes 65536 | tf_op jit(solution)/shard_map/all_to_all | solution.py:110
  327.6 5.8 %all-to-all-start.1 = ((f32[16,1,512,128]{3,2,1,0:T(8,128)}), f32[16,1,512,128]{3,2,1,0:T(8,128)}, u32[]{:S(2)}, u32[]{:S(2)}) async-start(f32[16,1,512,128]{3,2,1,0:T(8,128)} %bitcast.104), calls=%async_computation.1 | async-start | bytes 8388608 | tf_op jit(solution)/shard_map/all_to_all | solution.py:100
  337.1 167.9 %all-to-all-done.1 = f32[16,1,512,128]{3,2,1,0:T(8,128)} async-done(((f32[16,1,512,128]{3,2,1,0:T(8,128)}), f32[16,1,512,128]{3,2,1,0:T(8,128)}, u32[]{:S(2)}, u32[]{:S(2)}) %all-to-all-start.1) | async-done | bytes 4194336 | tf_op jit(solution)/shard_map/all_to_all | solution.py:100
  505.0 2.8 gather_fusion
  508.9 0.8 copy.77
  (166 shorter events, 41.8 us)
Async XLA Ops:
  6.5 327.1 %copy-start = (bf16[512,256]{1,0:T(8,128)(2,1)S(1)}, bf16[512,256]{1,0:T(8,128)(2,1)}, u32[]{:S(2)}) copy-start(bf16[512,256]{1,0:T(8,128)(2,1)} %param.11) | copy-start | bytes 786436
  6.5 85.6 %all-gather.2.cloned.1.call-start = ((), (), s32[]{:S(2)}) async-start(), calls=%async_computation.4 | async-start | bytes 4456448 | tf_op jit(solution)/shard_map/all_gather | solution.py:89
  9.2 95.0 %all-to-all-start = ((s32[16,1,2]{2,1,0:T(1,128)}), s32[16,1,2]{2,1,0:T(1,128)S(1)}, u32[]{:S(2)}, u32[]{:S(2)}) async-start(s32[16,1,2]{2,1,0:T(1,128)} %copy.66), calls=%async_computation | async-start | bytes 16384 | tf_op jit(solution)/shard_map/all_to_all | solution.py:88
  197.5 115.1 %all-to-all-start.2 = ((f32[16,1,512]{2,1,0:T(1,128)}), f32[16,1,512]{2,1,0:T(1,128)S(1)}, u32[]{:S(2)}, u32[]{:S(2)}) async-start(f32[16,1,512]{2,1,0:T(1,128)} %reshape.180), calls=%async_computation.2 | async-start | bytes 65536 | tf_op jit(solution)/shard_map/all_to_all | solution.py:107
  327.6 5.8 %copy-start.3 = (s32[1,2,3]{2,1,0:T(2,128)S(1)}, s32[1,2,3]{2,1,0:T(2,128)}, u32[]{:S(2)}) copy-start(s32[1,2,3]{2,1,0:T(2,128)} %param.15) | copy-start | bytes 76
  327.6 6.1 %copy-start.1 = (bf16[512,256]{1,0:T(8,128)(2,1)S(1)}, bf16[512,256]{1,0:T(8,128)(2,1)}, u32[]{:S(2)}) copy-start(bf16[512,256]{1,0:T(8,128)(2,1)} %param.10) | copy-start | bytes 786436
  327.6 177.4 %all-to-all-start.1 = ((f32[16,1,512,128]{3,2,1,0:T(8,128)}), f32[16,1,512,128]{3,2,1,0:T(8,128)}, u32[]{:S(2)}, u32[]{:S(2)}) async-start(f32[16,1,512,128]{3,2,1,0:T(8,128)} %bitcast.104), calls=%async_computation.1 | async-start | bytes 8388608 | tf_op jit(solution)/shard_map/all_to_all | solution.py:100
  334.1 1.0 copy-start.2
Sparse Core Ops, SparseCore 0:
  9.4 82.6 all-gather.1
where the time goes:
time: 519 us; the launch traced here: 517 us
  waiting for transfers between devices  235 us (45%)
  starting transfers between devices  125 us (24%)
  local copies, waits for them, and re-layouts  66 us (13%)
  matrix products  33.4 us (6%)
  other arithmetic  15.2 us (3%)
  blocking collectives  15 us (3%)
  loops' own time  13.7 us (3%)
  between operations  13.6 us (3%)
    all_to_all x1, waiting for transfers between devices, shards(): lax.all_to_all(summed_in.reshape(owners, slot_cap, tile_rows, head_dim),...  168 us
    all_to_all x1, starting transfers between devices, shards(): lax.all_to_all(top_in.reshape(owners, slot_cap, tile_rows), 'ctx', split_...  104 us
    all_gather x1, waiting for transfers between devices, shards(): lax.all_gather(queries, 'ctx', axis=0, tiled=True)  55 us
    dynamic_update_slice x48, local copies, waits for them, and re-layouts, shards(): lax.map(answer_tile, (source_of, request_in.reshape(-1, 2)))  23.9 us
    dot_general x7, matrix products, attend(): lax.dot_general(query, keys, (((1,), (1,)), ((), ())), preferred_element_...  19.8 us
    unnamed x15, local copies, waits for them, and re-layouts  18.2 us
    all_to_all x1, starting transfers between devices, shards(): lax.all_to_all(request_table, 'ctx', split_axis=0, concat_axis=0, tiled=T...  15.2 us
    all_to_all x1, blocking collectives, shards(): lax.all_to_all(total_in.reshape(owners, slot_cap, tile_rows), 'ctx', spli...  15 us
  transfers between devices with their start and end apart: 4, of which 3 were waited for; matrix products, arithmetic and copies ran while one was open for 6% of the time, Pallas kernels for 0%

commit v1 on v0

v1 whole, which is shorter than its diff:
```python
import functools
import math

import jax
import jax.numpy as jnp
from jax import lax
from jax.experimental import pallas as pl
from jax.experimental.pallas import tpu as pltpu
from jax.sharding import PartitionSpec as P

NEG = -1e30
LANES = 128
CHUNK = 1024
PIECE = 512
STRIP = 64
UNROLL = 2
NEAR = 6
FAR7 = (13, 15)
FAR8 = 14
WAVES = 1
UNITS = 2 * NEAR + 4
MESH = pl.DeviceIdType.MESH
F32 = jnp.float32
BF16 = jnp.bfloat16


def matmul(a, b):
    return lax.dot_general(a, b, (((1,), (0,)), ((), ())), preferred_element_type=F32)


def against(a, b):
    return lax.dot_general(a, b, (((1,), (1,)), ((), ())), preferred_element_type=F32)


def flipped(x):
    width = x.shape[1]
    rows = lax.broadcasted_iota(jnp.int32, (width, width), 0)
    columns = lax.broadcasted_iota(jnp.int32, (width, width), 1)
    eye = jnp.where(rows == columns, 1.0, 0.0).astype(BF16)
    return against(eye, x).astype(BF16)


def fold(x, op):
    return op(x.reshape(x.shape[0] // 8, 8, x.shape[1]), axis=0)


def mix(o1, l1, o2, l2):
    best = jnp.maximum(l1, l2)
    a = jnp.exp2(l1 - best)
    b = jnp.exp2(l2 - best)
    total = a + b
    part = 1.0 / total
    return o1 * (a * part) + o2 * (b * part), best + jnp.log2(total)


def slot(side, d):
    return 2 * d - 1 + side


def kernel(
    ranks, rate,
    picks, q_in, ko_in, vo_in, k_in, v_in,
    out,
    q_own, k_own, v_own, vt_own, keys, values, kt, vw,
    qt, tab, qm, s_a, s_b, m_a, m_b, acc,
    part, plse, mine, mlse,
    sel7, sel8, pass8,
    od8, od7, a8, a8l, b8, b8l, b7, b7l, chain, clse,
    load_sem, q_send, q_recv, t_send, t_recv, f_send, f_recv, c_send, c_recv,
):
    z = lax.axis_index("ctx")
    after = lax.rem(z + 1, ranks)
    before = lax.rem(z + ranks - 1, ranks)
    rows = q_own.shape[0]
    span = rows // WAVES
    blocks = span // LANES
    half = blocks // 2
    n_chunks = keys.shape[0] // CHUNK
    lane = lax.broadcasted_iota(jnp.int32, (8, LANES), 1)

    loads = [
        pltpu.make_async_copy(source, target, load_sem.at[i])
        for i, (source, target) in enumerate(
            [(q_in, q_own), (k_in, keys), (v_in, values), (ko_in, k_own), (vo_in, v_own)]
        )
    ]
    for load in loads:
        load.start()

    barrier = pltpu.get_barrier_semaphore()
    for peer in (before, after):
        pl.semaphore_signal(barrier, inc=1, device_id={"ctx": peer}, device_id_type=MESH)

    def remote(source, target, send, recv, peer):
        return pltpu.make_async_remote_copy(
            src_ref=source, dst_ref=target, send_sem=send, recv_sem=recv,
            device_id={"ctx": peer}, device_id_type=MESH,
        )

    def outward(side):
        return after if side == 0 else before

    def inward(side):
        return before if side == 0 else after

    def q_copy(w, side, d, h):
        source = 0 if d == 1 else slot(side, d - 1)
        return remote(
            qt.at[w, source, h], qt.at[w, slot(side, d), h],
            q_send.at[w, side, d - 1, h], q_recv.at[w, side, d - 1, h], outward(side),
        )

    def t_copy(side, d):
        source = 0 if d == 1 else slot(side, d - 1) if d <= NEAR + 1 else FAR7[side]
        target = slot(side, d) if d <= NEAR else FAR7[side] if d == NEAR + 1 else FAR8
        return remote(tab.at[source], tab.at[target], t_send.at[side, d - 1], t_recv.at[side, d - 1], outward(side))

    def sel7_copy(w, side):
        return remote(
            sel7.at[w, side], qt.at[w, FAR7[side], 0],
            q_send.at[w, side, 6, 0], q_recv.at[w, side, 6, 0], outward(side),
        )

    def sel8_copy(w, side):
        return remote(
            sel8.at[w, side], pass8.at[w, side], q_send.at[w, side, 6, 1], q_recv.at[w, side, 6, 1], outward(side)
        )

    def pass8_copy(w, side):
        return remote(
            pass8.at[w, side],
            qt.at[w, FAR8, 0, pl.ds(side * half * LANES, half * LANES)],
            q_send.at[w, side, 7, 0], q_recv.at[w, side, 7, 0], outward(side),
        )

    def far_copy(w, side, i, source, target):
        return remote(source, target, f_send.at[w, side, i], f_recv.at[w, side, i], inward(side))

    def far8_copies(w, side):
        return [
            far_copy(w, side, 0, od8.at[w, pl.ds(side * half, half)], a8.at[w, side]),
            far_copy(w, side, 1, plse.at[w, FAR8], a8l.at[w, side]),
        ]

    def far8_passes(w, side):
        return [
            far_copy(w, side, 2, a8.at[w, side], b8.at[w, side]),
            far_copy(w, side, 3, a8l.at[w, side], b8l.at[w, side]),
        ]

    def far7_copies(w, side):
        return [
            far_copy(w, side, 4, od7.at[w, side], b7.at[w, side]),
            far_copy(w, side, 5, plse.at[w, FAR7[side]], b7l.at[w, side]),
        ]

    def chain_copies(w, side, d, h):
        return [
            remote(
                ref.at[w, side, d, h], ref.at[w, side, d - 1, h],
                c_send.at[w, side, d - 1, h, i], c_recv.at[w, side, d - 1, h, i], inward(side),
            )
            for i, ref in enumerate((chain, clse))
        ]

    def chosen(u, index):
        found = jnp.sum(jnp.where(lane == index, tab[u], 0.0), axis=1, keepdims=True)
        return jnp.broadcast_to(found, (8, LANES))[0:1, :]

    def is_head(want, h):
        return jnp.where(want == float(h + 1), 1.0, 0.0)

    def columns(j):
        return pl.ds(j * LANES, LANES)

    table = jnp.zeros((8, LANES), F32)
    for h in range(2):
        for k in range(3):
            table = jnp.where(lane == picks[0, h, k], float(h + 1), table)
    tab[0] = table

    loads[0].wait()
    for h in range(2):
        for w in range(WAVES):
            qt[w, 0, h] = q_own[w * span:(w + 1) * span, columns(h)]
    pl.semaphore_wait(barrier, 2)
    for side in range(2):
        t_copy(side, 1).start()
    for w in range(WAVES):
        for h in range(2):
            for side in range(2):
                q_copy(w, side, 1, h).start()

    def build(w, u):
        want = chosen(u, z)
        several = jnp.where(u < FAR7[0], 1, 0)
        for h in range(2):
            qm[:, columns(h)] = qt[w, u, h * several] * is_head(want, h).astype(BF16)

    def score(c, i, s_ref, m_ref):
        s = matmul(qm[...], kt[c, :, i * PIECE:(i + 1) * PIECE])
        for r in range(0, span, STRIP):
            strip = s[r:r + STRIP]
            s_ref[c, r:r + STRIP, i * PIECE:(i + 1) * PIECE] = strip
            top = m_ref[r:r + STRIP, :]
            for j in range(0, PIECE, LANES):
                top = jnp.maximum(top, strip[:, j:j + LANES])
            m_ref[r:r + STRIP, :] = top

    def weigh(c, first, last, s_ref, m_ref):
        strips = []
        for r in range(first, last, STRIP):
            top = jnp.concatenate([m_ref[r:r + STRIP, :]] * (CHUNK // LANES), axis=1)
            strips.append(jnp.exp2((s_ref[c, r:r + STRIP, :] - top) * rate).astype(BF16))
        return strips

    def absorb(c, strips, keep):
        at = pl.ds(pl.multiple_of(c * CHUNK, CHUNK), CHUNK)
        vw[c, :, 0:LANES] = values[at, 0:LANES] * keep[0] + values[at, LANES:2 * LANES] * keep[1]
        acc[...] += matmul(jnp.concatenate(strips, axis=0), vw[c])

    def chunks(body):
        def several(i, _):
            for k in range(UNROLL):
                body(i * UNROLL + k)
            return 0

        lax.fori_loop(0, n_chunks // UNROLL, several, 0)

    def lowest(m_ref):
        m_ref[...] = jnp.full((span, LANES), NEG, F32)

    def spread(m_ref):
        m_ref[...] = jnp.broadcast_to(jnp.max(m_ref[...], axis=1, keepdims=True), (span, LANES))

    def keepers(u):
        want = chosen(u, z)
        return [is_head(want, h).astype(BF16) for h in range(2)]

    def finish(w, u, m_ref):
        across = lax.broadcasted_iota(jnp.int32, (LANES, LANES), 1)
        packed = jnp.zeros((LANES, LANES), F32)
        for j in range(blocks):
            cut = slice(j * LANES, (j + 1) * LANES)
            total = acc[cut, LANES:2 * LANES]
            part[w, u, j] = jnp.transpose(acc[cut, 0:LANES] * (1.0 / total))
            packed = jnp.where(across == 8 * j, m_ref[cut, :] * rate + jnp.log2(total), packed)
        packed = jnp.transpose(packed)
        for j in range(blocks):
            plse[w, u, j:j + 1, :] = packed[8 * j:8 * j + 1, :]

    def only_score(w, u, s_ref, m_ref):
        build(w, u)
        lowest(m_ref)

        def body(c):
            for i in range(CHUNK // PIECE):
                score(c, i, s_ref, m_ref)

        chunks(body)
        spread(m_ref)

    def phase(g, s_new, m_new, s_old, m_old):
        w, u = g // UNITS, lax.rem(g, UNITS)
        w_old, u_old = (g - 1) // UNITS, lax.rem(g - 1, UNITS)
        build(w, u)
        lowest(m_new)
        keep = keepers(u_old)
        acc[...] = jnp.zeros_like(acc)

        def body(c):
            strips = []
            parts = CHUNK // PIECE
            for i in range(parts):
                score(c, i, s_new, m_new)
                strips += weigh(c, i * span // parts, (i + 1) * span // parts, s_old, m_old)
            absorb(c, strips, keep)

        chunks(body)
        finish(w_old, u_old, m_old)
        spread(m_new)

    def only_weigh(w, u, s_old, m_old):
        keep = keepers(u)
        acc[...] = jnp.zeros_like(acc)
        chunks(lambda c: absorb(c, weigh(c, 0, span, s_old, m_old), keep))
        finish(w, u, m_old)

    def relay(w, d, h):
        for side in range(2):
            q_copy(w, side, d, h).wait_recv()
            if d < NEAR:
                q_copy(w, side, d + 1, h).start()
            if w == 0 and h == 0:
                t_copy(side, d).wait_recv()
                t_copy(side, d + 1).start()

    def wanted(side):
        u = slot(side, NEAR)
        step = 1 if side == 0 else ranks - 1
        return [chosen(u, lax.rem(z + i * step, ranks)) for i in range(3)]

    def narrow(w):
        for side in range(2):
            _, want7, want8 = wanted(side)
            first, second = (qt[w, slot(side, NEAR), h] for h in range(2))
            sel7[w, side] = first * is_head(want7, 0).astype(BF16) + second * is_head(want7, 1).astype(BF16)
            cut = slice(side * half * LANES, (side + 1) * half * LANES)
            sel8[w, side] = first[cut] * is_head(want8, 0).astype(BF16) + second[cut] * is_head(want8, 1).astype(BF16)
            sel8_copy(w, side).start()
            sel7_copy(w, side).start()

    def pass_on(w):
        for side in range(2):
            sel8_copy(w, side).wait_recv()
            pass8_copy(w, side).start()
        if w == 0:
            for side in range(2):
                t_copy(side, 7).wait_recv()
            t_copy(0, 8).start()
        for side in range(2):
            sel7_copy(w, side).wait_recv()

    def arrive(w):
        if w == 0:
            t_copy(0, 8).wait_recv()
        for side in range(2):
            pass8_copy(w, side).wait_recv()

    def give7(w, side):
        od7[w, side] = part[w, FAR7[side]].astype(BF16)
        for copy in far7_copies(w, side):
            copy.start()

    def give8(w):
        od8[w] = part[w, FAR8].astype(BF16)
        for side in range(2):
            for copy in far8_copies(w, side):
                copy.start()

    def pass_back(w):
        for side in range(2):
            for copy in far8_copies(w, side):
                copy.wait_recv()
            for copy in far8_passes(w, side):
                copy.start()

    def own_lse(want, h, w, u, j):
        return jnp.where(want == float(h + 1), plse[w, u, j:j + 1, :], NEG)

    def gather6(w, h):
        for side in range(2):
            if h == 0:
                for copy in far7_copies(w, side) + far8_passes(w, side):
                    copy.wait_recv()
            u = slot(side, NEAR)
            want6, want7, want8 = wanted(side)
            for j in range(blocks):
                o, lse = mix(
                    part[w, u, j], own_lse(want6, h, w, u, j),
                    b7[w, side, j].astype(F32), jnp.where(want7 == float(h + 1), b7l[w, side, j:j + 1, :], NEG),
                )
                if j // half == side:
                    o, lse = mix(
                        o, lse, b8[w, side, j % half].astype(F32),
                        jnp.where(want8 == float(h + 1), b8l[w, side, j:j + 1, :], NEG),
                    )
                chain[w, side, NEAR, h, j] = o.astype(BF16)
                clse[w, side, NEAR, h, j:j + 1, :] = lse
            for copy in chain_copies(w, side, NEAR, h):
                copy.start()

    def back(w, d, h):
        for side in range(2):
            for copy in chain_copies(w, side, d + 1, h):
                copy.wait_recv()
            u = slot(side, d)
            want = chosen(u, z)
            for j in range(blocks):
                o, lse = mix(
                    chain[w, side, d, h, j].astype(F32), clse[w, side, d, h, j:j + 1, :],
                    part[w, u, j], own_lse(want, h, w, u, j),
                )
                chain[w, side, d, h, j] = o.astype(BF16)
                clse[w, side, d, h, j:j + 1, :] = lse
            for copy in chain_copies(w, side, d, h):
                copy.start()

    def final(w, h):
        for side in range(2):
            for copy in chain_copies(w, side, 1, h):
                copy.wait_recv()
        for j in range(blocks):
            at = w * blocks + j
            o, lse = mine[h, at], mlse[h, at:at + 1, :]
            for side in range(2):
                o, lse = mix(o, lse, chain[w, side, 0, h, j].astype(F32), clse[w, side, 0, h, j:j + 1, :])
            out[columns(at), columns(h)] = jnp.transpose(o).astype(BF16)

    def causal(h):
        key_at = lax.broadcasted_iota(jnp.int32, (rows, span), 0)
        query_at = lax.broadcasted_iota(jnp.int32, (rows, span), 1)
        vt_own[h] = flipped(v_own[:, columns(h)])
        want = chosen(0, z)
        for w in range(WAVES):
            s = jnp.where(key_at <= query_at + w * span, against(k_own[:, columns(h)], qt[w, 0, h]), NEG)
            top = jnp.max(fold(s, jnp.max), axis=0, keepdims=True)
            p = jnp.exp2((s - top) * rate)
            total = jnp.sum(fold(p, jnp.sum), axis=0, keepdims=True)
            o = matmul(vt_own[h], p.astype(BF16)) * (1.0 / total)
            lse = top * rate + jnp.log2(total)
            for j in range(blocks):
                cut = slice(j * LANES, (j + 1) * LANES)
                at = w * blocks + j
                mixed, both = mix(o[:, cut], lse[:, cut], part[w, 0, j], own_lse(want, h, w, 0, j))
                mine[h, at] = mixed
                mlse[h, at:at + 1, :] = both

    steps = {}

    def place(g, step, *args):
        steps.setdefault(g, []).append(functools.partial(step, *args))

    for d in range(2, NEAR + 1):
        for h in range(2):
            place(2 * d - 3 + h, relay, 0, d, h)
    place(2 * NEAR - 2, narrow, 0)
    place(13, pass_on, 0)
    place(14, arrive, 0)
    place(15, give7, 0, 0)

    def run(g):
        for k in sorted(steps):
            if k % 2 == g[1]:

                @pl.when(g[0] == k)
                def _(k=k):
                    for step in steps[k]:
                        step()

    for c in range(n_chunks):
        vw[c, :, LANES:2 * LANES] = jnp.ones((CHUNK, LANES), BF16)
    loads[1].wait()
    for c in range(n_chunks):
        kt[c] = flipped(keys[c * CHUNK:(c + 1) * CHUNK, :])
    only_score(0, 0, s_a, m_a)
    loads[2].wait()
    for h in range(2):
        relay(0, 1, h)

    def pair(i, _):
        run((2 * i - 1, 1))
        phase(2 * i - 1, s_b, m_b, s_a, m_a)
        run((2 * i, 0))
        phase(2 * i, s_a, m_a, s_b, m_b)
        return 0

    last = WAVES * UNITS - 1
    lax.fori_loop(1, (last + 1) // 2, pair, 0)
    for step in steps[last]:
        step()
    phase(last, s_b, m_b, s_a, m_a)
    give8(0)
    only_weigh(0, UNITS - 1, s_b, m_b)
    give7(0, 1)
    pass_back(0)
    for load in loads[3:]:
        load.wait()
    for h in range(2):
        causal(h)
    for h in range(2):
        gather6(0, h)
    for d in range(NEAR - 1, 0, -1):
        for h in range(2):
            back(0, d, h)
    for h in range(2):
        final(0, h)

    for side in range(2):
        for d in range(1, NEAR + 2):
            t_copy(side, d).wait_send()
    t_copy(0, 8).wait_send()
    for w in range(WAVES):
        for side in range(2):
            for h in range(2):
                for d in range(1, NEAR + 1):
                    q_copy(w, side, d, h).wait_send()
                    for copy in chain_copies(w, side, d, h):
                        copy.wait_send()
            for copy in [sel7_copy(w, side), sel8_copy(w, side), pass8_copy(w, side)]:
                copy.wait_send()
            for copy in far8_copies(w, side) + far8_passes(w, side) + far7_copies(w, side):
                copy.wait_send()


def shards(queries, keys_own, values_own, keys_cache, values_cache, picks):
    ranks = lax.axis_size("ctx")
    rows, width = queries.shape
    depth = keys_cache.shape[0]
    span = rows // WAVES
    blocks = span // LANES
    half = blocks // 2
    rate = (width // 2) ** (-0.5) * math.log2(math.e)
    return pl.pallas_call(
        functools.partial(kernel, ranks, rate),
        out_shape=jax.ShapeDtypeStruct((rows, width), BF16),
        in_specs=[pl.BlockSpec(memory_space=pltpu.SMEM)] + [pl.BlockSpec(memory_space=pl.ANY)] * 5,
        out_specs=pl.BlockSpec(memory_space=pltpu.VMEM),
        scratch_shapes=[
            pltpu.VMEM((rows, width), BF16),
            pltpu.VMEM((rows, width), BF16),
            pltpu.VMEM((rows, width), BF16),
            pltpu.VMEM((2, LANES, rows), BF16),
            pltpu.VMEM((depth, width), BF16),
            pltpu.VMEM((depth, width), BF16),
            pltpu.VMEM((depth // CHUNK, width, CHUNK), BF16),
            pltpu.VMEM((depth // CHUNK, CHUNK, width), BF16),
            pltpu.VMEM((WAVES, UNITS, 2, span, LANES), BF16),
            pltpu.VMEM((UNITS, 8, LANES), F32),
            pltpu.VMEM((span, width), BF16),
            pltpu.VMEM((depth // CHUNK, span, CHUNK), F32),
            pltpu.VMEM((depth // CHUNK, span, CHUNK), F32),
            pltpu.VMEM((span, LANES), F32),
            pltpu.VMEM((span, LANES), F32),
            pltpu.VMEM((span, width), F32),
            pltpu.VMEM((WAVES, UNITS, blocks, LANES, LANES), F32),
            pltpu.VMEM((WAVES, UNITS, blocks, LANES), F32),
            pltpu.VMEM((2, WAVES * blocks, LANES, LANES), F32),
            pltpu.VMEM((2, WAVES * blocks, LANES), F32),
            pltpu.VMEM((WAVES, 2, span, LANES), BF16),
            pltpu.VMEM((WAVES, 2, span // 2, LANES), BF16),
            pltpu.VMEM((WAVES, 2, span // 2, LANES), BF16),
            pltpu.VMEM((WAVES, blocks, LANES, LANES), BF16),
            pltpu.VMEM((WAVES, 2, blocks, LANES, LANES), BF16),
            pltpu.VMEM((WAVES, 2, half, LANES, LANES), BF16),
            pltpu.VMEM((WAVES, 2, blocks, LANES), F32),
            pltpu.VMEM((WAVES, 2, half, LANES, LANES), BF16),
            pltpu.VMEM((WAVES, 2, blocks, LANES), F32),
            pltpu.VMEM((WAVES, 2, blocks, LANES, LANES), BF16),
            pltpu.VMEM((WAVES, 2, blocks, LANES), F32),
            pltpu.VMEM((WAVES, 2, NEAR + 1, 2, blocks, LANES, LANES), BF16),
            pltpu.VMEM((WAVES, 2, NEAR + 1, 2, blocks, LANES), F32),
            pltpu.SemaphoreType.DMA((5,)),
            pltpu.SemaphoreType.DMA((WAVES, 2, 8, 2)),
            pltpu.SemaphoreType.DMA((WAVES, 2, 8, 2)),
            pltpu.SemaphoreType.DMA((2, 8)),
            pltpu.SemaphoreType.DMA((2, 8)),
            pltpu.SemaphoreType.DMA((WAVES, 2, 6)),
            pltpu.SemaphoreType.DMA((WAVES, 2, 6)),
            pltpu.SemaphoreType.DMA((WAVES, 2, NEAR, 2, 2)),
            pltpu.SemaphoreType.DMA((WAVES, 2, NEAR, 2, 2)),
        ],
        compiler_params=pltpu.CompilerParams(
            collective_id=0, has_side_effects=True, vmem_limit_bytes=56 * 1024 * 1024
        ),
        cost_estimate=pl.CostEstimate(
            flops=4 * 16 * depth * rows * width, bytes_accessed=2 * (2 * depth + 4 * rows) * width,
            transcendentals=16 * depth * rows,
        ),
    )(picks, queries, keys_own, values_own, keys_cache, values_cache)


def solution(mesh):
    placed = P(("req", "ctx"), "head")
    return jax.shard_map(
        shards,
        mesh=mesh,
        in_specs=(placed,) * 5 + (P(("req", "ctx"), "head", None),),
        out_specs=placed,
        check_vma=False,
    )
```

time: 519 us -> 119 us (0.23)
  the two profiles are of different devices: /device:TPU:40 before, /device:TPU:26 now
where the time goes in v1:
time: 119 us
  Pallas kernels  118 us (99%)
  local copies, waits for them, and re-layouts  1.67 us (1%)
    pallas_call x1, Pallas kernels, shards(): pl.pallas_call(functools.partial(kernel, ranks, rate), out_shape=jax.Shap...  118 us

profile of v1, /device:TPU:26, one launch (start us, length us, event | category | flops | bytes accessed | tf_op | source)
XLA Modules:
  0.0 119.3 jit_solution(16990177551918079649)
XLA Ops:
  0.0 117.6 %shard_map.64 = bf16[512,256]{1,0:T(8,128)(2,1)} custom-call(s32[1,2,3]{2,1,0:T(2,128)} %picks.1, bf16[512,256]{1,0:T(8,128)(2,1)} %q_in.1, bf16[512,256]{1,0:T(8,128)(2,1)} %ko_in.1, bf16[512,256]{1,0:T(8,128)(2,1)} %vo_in.1, bf16[4096,256]{1,0:T(8,128)(2,1)} %k_in.1, bf16[4096,256]{1,0:T(8,128)(2,1)} %v_in.1), custom_call_target="tpu_custom_call" | custom-call | flops 34359738368 | bytes 5242880 | tf_op jit(solution)/shard_map/pallas_call | solution.py:504
  117.7 1.7 %copy.8 = bf16[512,256]{1,0:T(8,128)(2,1)} copy(bf16[512,256]{1,0:T(8,128)(2,1)} %shard_map.64) | data formatting | bytes 524288

commit v2 on v1

--- a/solution.py
+++ b/solution.py
@@ -15,8 +15,8 @@
 STRIP = 64
 UNROLL = 2
 NEAR = 6
-FAR7 = (13, 15)
-FAR8 = 14
+FAR8 = 13
+FAR7 = (14, 15)
 WAVES = 1
 UNITS = 2 * NEAR + 4
 MESH = pl.DeviceIdType.MESH
@@ -103,11 +103,14 @@
     def inward(side):
         return before if side == 0 else after
 
-    def q_copy(w, side, d, h):
+    def cut(r):
+        return pl.ds(r * half * LANES, half * LANES)
+
+    def q_copy(w, side, d, h, r):
         source = 0 if d == 1 else slot(side, d - 1)
         return remote(
-            qt.at[w, source, h], qt.at[w, slot(side, d), h],
-            q_send.at[w, side, d - 1, h], q_recv.at[w, side, d - 1, h], outward(side),
+            qt.at[w, source, h, cut(r)], qt.at[w, slot(side, d), h, cut(r)],
+            q_send.at[w, side, d - 1, h, r], q_recv.at[w, side, d - 1, h, r], outward(side),
         )
 
     def t_copy(side, d):
@@ -115,22 +118,22 @@
         target = slot(side, d) if d <= NEAR else FAR7[side] if d == NEAR + 1 else FAR8
         return remote(tab.at[source], tab.at[target], t_send.at[side, d - 1], t_recv.at[side, d - 1], outward(side))
 
-    def sel7_copy(w, side):
+    def sel7_copy(w, side, r):
         return remote(
-            sel7.at[w, side], qt.at[w, FAR7[side], 0],
-            q_send.at[w, side, 6, 0], q_recv.at[w, side, 6, 0], outward(side),
+            sel7.at[w, side, cut(r)], qt.at[w, FAR7[side], 0, cut(r)],
+            q_send.at[w, side, 6, 0, r], q_recv.at[w, side, 6, 0, r], outward(side),
         )
 
     def sel8_copy(w, side):
         return remote(
-            sel8.at[w, side], pass8.at[w, side], q_send.at[w, side, 6, 1], q_recv.at[w, side, 6, 1], outward(side)
+            sel8.at[w, side], pass8.at[w, side], q_send.at[w, side, 6, 1, 0], q_recv.at[w, side, 6, 1, 0], outward(side)
         )
 
     def pass8_copy(w, side):
         return remote(
             pass8.at[w, side],
-            qt.at[w, FAR8, 0, pl.ds(side * half * LANES, half * LANES)],
-            q_send.at[w, side, 7, 0], q_recv.at[w, side, 7, 0], outward(side),
+            qt.at[w, FAR8, 0, cut(side)],
+            q_send.at[w, side, 7, 0, 0], q_recv.at[w, side, 7, 0, 0], outward(side),
         )
 
     def far_copy(w, side, i, source, target):
@@ -154,11 +157,11 @@
             far_copy(w, side, 5, plse.at[w, FAR7[side]], b7l.at[w, side]),
         ]
 
-    def chain_copies(w, side, d, h):
+    def chain_copies(w, side, d, h, r):
         return [
             remote(
-                ref.at[w, side, d, h], ref.at[w, side, d - 1, h],
-                c_send.at[w, side, d - 1, h, i], c_recv.at[w, side, d - 1, h, i], inward(side),
+                ref.at[w, side, d, h, r], ref.at[w, side, d - 1, h, r],
+                c_send.at[w, side, d - 1, h, r, i], c_recv.at[w, side, d - 1, h, r, i], inward(side),
             )
             for i, ref in enumerate((chain, clse))
         ]
@@ -186,14 +189,13 @@
     pl.semaphore_wait(barrier, 2)
     for side in range(2):
         t_copy(side, 1).start()
-    for w in range(WAVES):
-        for h in range(2):
-            for side in range(2):
-                q_copy(w, side, 1, h).start()
+    for i in range(4):
+        for side in range(2):
+            q_copy(0, side, 1, i % 2, (i // 2) ^ side).start()
 
     def build(w, u):
         want = chosen(u, z)
-        several = jnp.where(u < FAR7[0], 1, 0)
+        several = jnp.where(u < FAR8, 1, 0)
         for h in range(2):
             qm[:, columns(h)] = qt[w, u, h * several] * is_head(want, h).astype(BF16)
 
@@ -219,8 +221,10 @@
         vw[c, :, 0:LANES] = values[at, 0:LANES] * keep[0] + values[at, LANES:2 * LANES] * keep[1]
         acc[...] += matmul(jnp.concatenate(strips, axis=0), vw[c])
 
-    def chunks(body):
+    def chunks(body, middle=None):
         def several(i, _):
+            if middle is not None:
+                pl.when(i == 1)(middle)
             for k in range(UNROLL):
                 body(i * UNROLL + k)
             return 0
@@ -260,7 +264,7 @@
         chunks(body)
         spread(m_ref)
 
-    def phase(g, s_new, m_new, s_old, m_old):
+    def phase(g, parity, s_new, m_new, s_old, m_old):
         w, u = g // UNITS, lax.rem(g, UNITS)
         w_old, u_old = (g - 1) // UNITS, lax.rem(g - 1, UNITS)
         build(w, u)
@@ -276,7 +280,7 @@
                 strips += weigh(c, i * span // parts, (i + 1) * span // parts, s_old, m_old)
             absorb(c, strips, keep)
 
-        chunks(body)
+        chunks(body, functools.partial(run, g, parity, 1))
         finish(w_old, u_old, m_old)
         spread(m_new)
 
@@ -286,12 +290,13 @@
         chunks(lambda c: absorb(c, weigh(c, 0, span, s_old, m_old), keep))
         finish(w, u, m_old)
 
-    def relay(w, d, h):
-        for side in range(2):
-            q_copy(w, side, d, h).wait_recv()
+    def relay(w, d, i):
+        for side in range(2):
+            h, r = i % 2, (i // 2) ^ side
+            q_copy(w, side, d, h, r).wait_recv()
             if d < NEAR:
-                q_copy(w, side, d + 1, h).start()
-            if w == 0 and h == 0:
+                q_copy(w, side, d + 1, h, r).start()
+            if i == 0:
                 t_copy(side, d).wait_recv()
                 t_copy(side, d + 1).start()
 
@@ -300,32 +305,34 @@
         step = 1 if side == 0 else ranks - 1
         return [chosen(u, lax.rem(z + i * step, ranks)) for i in range(3)]
 
-    def narrow(w):
+    def narrow(w, i):
         for side in range(2):
             _, want7, want8 = wanted(side)
-            first, second = (qt[w, slot(side, NEAR), h] for h in range(2))
-            sel7[w, side] = first * is_head(want7, 0).astype(BF16) + second * is_head(want7, 1).astype(BF16)
-            cut = slice(side * half * LANES, (side + 1) * half * LANES)
-            sel8[w, side] = first[cut] * is_head(want8, 0).astype(BF16) + second[cut] * is_head(want8, 1).astype(BF16)
-            sel8_copy(w, side).start()
-            sel7_copy(w, side).start()
+            r = i ^ side
+            rows_of = slice(r * half * LANES, (r + 1) * half * LANES)
+            first, second = (qt[w, slot(side, NEAR), h, rows_of] for h in range(2))
+            if i == 0:
+                sel8[w, side] = first * is_head(want8, 0).astype(BF16) + second * is_head(want8, 1).astype(BF16)
+                sel8_copy(w, side).start()
+            sel7[w, side, rows_of] = first * is_head(want7, 0).astype(BF16) + second * is_head(want7, 1).astype(BF16)
+            sel7_copy(w, side, r).start()
 
     def pass_on(w):
         for side in range(2):
             sel8_copy(w, side).wait_recv()
             pass8_copy(w, side).start()
-        if w == 0:
-            for side in range(2):
-                t_copy(side, 7).wait_recv()
-            t_copy(0, 8).start()
-        for side in range(2):
-            sel7_copy(w, side).wait_recv()
-
-    def arrive(w):
-        if w == 0:
-            t_copy(0, 8).wait_recv()
+        for side in range(2):
+            t_copy(side, 7).wait_recv()
+        t_copy(0, 8).start()
+
+    def arrive8(w):
+        t_copy(0, 8).wait_recv()
         for side in range(2):
             pass8_copy(w, side).wait_recv()
+
+    def arrive7(w, side):
+        for r in range(2):
+            sel7_copy(w, side, r).wait_recv()
 
     def give7(w, side):
         od7[w, side] = part[w, FAR7[side]].astype(BF16)
@@ -348,53 +355,54 @@
     def own_lse(want, h, w, u, j):
         return jnp.where(want == float(h + 1), plse[w, u, j:j + 1, :], NEG)
 
-    def gather6(w, h):
-        for side in range(2):
-            if h == 0:
-                for copy in far7_copies(w, side) + far8_passes(w, side):
-                    copy.wait_recv()
-            u = slot(side, NEAR)
-            want6, want7, want8 = wanted(side)
-            for j in range(blocks):
-                o, lse = mix(
-                    part[w, u, j], own_lse(want6, h, w, u, j),
-                    b7[w, side, j].astype(F32), jnp.where(want7 == float(h + 1), b7l[w, side, j:j + 1, :], NEG),
-                )
-                if j // half == side:
+    def gather6(w, side):
+        for copy in far7_copies(w, side) + far8_passes(w, side):
+            copy.wait_recv()
+        u = slot(side, NEAR)
+        want6, want7, want8 = wanted(side)
+        for r in range(2):
+            for h in range(2):
+                for k in range(half):
+                    j = r * half + k
                     o, lse = mix(
-                        o, lse, b8[w, side, j % half].astype(F32),
-                        jnp.where(want8 == float(h + 1), b8l[w, side, j:j + 1, :], NEG),
+                        part[w, u, j], own_lse(want6, h, w, u, j),
+                        b7[w, side, j].astype(F32), jnp.where(want7 == float(h + 1), b7l[w, side, j:j + 1, :], NEG),
                     )
-                chain[w, side, NEAR, h, j] = o.astype(BF16)
-                clse[w, side, NEAR, h, j:j + 1, :] = lse
-            for copy in chain_copies(w, side, NEAR, h):
-                copy.start()
-
-    def back(w, d, h):
-        for side in range(2):
-            for copy in chain_copies(w, side, d + 1, h):
+                    if r == side:
+                        o, lse = mix(
+                            o, lse, b8[w, side, k].astype(F32),
+                            jnp.where(want8 == float(h + 1), b8l[w, side, j:j + 1, :], NEG),
+                        )
+                    chain[w, side, NEAR, h, r, k] = o.astype(BF16)
+                    clse[w, side, NEAR, h, r, k:k + 1, :] = lse
+                for copy in chain_copies(w, side, NEAR, h, r):
+                    copy.start()
+
+    def back(w, d, h, r):
+        for side in range(2):
+            for copy in chain_copies(w, side, d + 1, h, r):
                 copy.wait_recv()
             u = slot(side, d)
             want = chosen(u, z)
-            for j in range(blocks):
+            for k in range(half):
                 o, lse = mix(
-                    chain[w, side, d, h, j].astype(F32), clse[w, side, d, h, j:j + 1, :],
-                    part[w, u, j], own_lse(want, h, w, u, j),
+                    chain[w, side, d, h, r, k].astype(F32), clse[w, side, d, h, r, k:k + 1, :],
+                    part[w, u, r * half + k], own_lse(want, h, w, u, r * half + k),
                 )
-                chain[w, side, d, h, j] = o.astype(BF16)
-                clse[w, side, d, h, j:j + 1, :] = lse
-            for copy in chain_copies(w, side, d, h):
+                chain[w, side, d, h, r, k] = o.astype(BF16)
+                clse[w, side, d, h, r, k:k + 1, :] = lse
+            for copy in chain_copies(w, side, d, h, r):
                 copy.start()
 
-    def final(w, h):
-        for side in range(2):
-            for copy in chain_copies(w, side, 1, h):
+    def final(w, h, r):
+        for side in range(2):
+            for copy in chain_copies(w, side, 1, h, r):
                 copy.wait_recv()
-        for j in range(blocks):
-            at = w * blocks + j
+        for k in range(half):
+            at = w * blocks + r * half + k
             o, lse = mine[h, at], mlse[h, at:at + 1, :]
             for side in range(2):
-                o, lse = mix(o, lse, chain[w, side, 0, h, j].astype(F32), clse[w, side, 0, h, j:j + 1, :])
+                o, lse = mix(o, lse, chain[w, side, 0, h, r, k].astype(F32), clse[w, side, 0, h, r, k:k + 1, :])
             out[columns(at), columns(h)] = jnp.transpose(o).astype(BF16)
 
     def causal(h):
@@ -422,18 +430,21 @@
         steps.setdefault(g, []).append(functools.partial(step, *args))
 
     for d in range(2, NEAR + 1):
-        for h in range(2):
-            place(2 * d - 3 + h, relay, 0, d, h)
-    place(2 * NEAR - 2, narrow, 0)
-    place(13, pass_on, 0)
-    place(14, arrive, 0)
-    place(15, give7, 0, 0)
-
-    def run(g):
+        for i in range(4):
+            place(2 * (2 * d - 3) + i, relay, 0, d, i)
+    place(2 * (2 * NEAR - 3) + 1, narrow, 0, 0)
+    place(2 * (2 * NEAR - 3) + 3, narrow, 0, 1)
+    place(2 * 11 + 1, pass_on, 0)
+    place(2 * FAR8, arrive8, 0)
+    place(2 * FAR7[0], arrive7, 0, 0)
+    place(2 * FAR7[1], arrive7, 0, 1)
+    place(2 * FAR7[1], give8, 0)
+
+    def run(g, parity, middle):
         for k in sorted(steps):
-            if k % 2 == g[1]:
-
-                @pl.when(g[0] == k)
+            if k % 2 == middle and (k // 2) % 2 == parity:
+
+                @pl.when(g == k // 2)
                 def _(k=k):
                     for step in steps[k]:
                         step()
@@ -445,36 +456,36 @@
         kt[c] = flipped(keys[c * CHUNK:(c + 1) * CHUNK, :])
     only_score(0, 0, s_a, m_a)
     loads[2].wait()
-    for h in range(2):
-        relay(0, 1, h)
+    for i in range(4):
+        relay(0, 1, i)
 
     def pair(i, _):
-        run((2 * i - 1, 1))
-        phase(2 * i - 1, s_b, m_b, s_a, m_a)
-        run((2 * i, 0))
-        phase(2 * i, s_a, m_a, s_b, m_b)
+        run(2 * i - 1, 1, 0)
+        phase(2 * i - 1, 1, s_b, m_b, s_a, m_a)
+        run(2 * i, 0, 0)
+        phase(2 * i, 0, s_a, m_a, s_b, m_b)
         return 0
 
-    last = WAVES * UNITS - 1
-    lax.fori_loop(1, (last + 1) // 2, pair, 0)
-    for step in steps[last]:
+    lax.fori_loop(1, UNITS // 2, pair, 0)
+    for step in steps[2 * (UNITS - 1)]:
         step()
-    phase(last, s_b, m_b, s_a, m_a)
-    give8(0)
+    phase(UNITS - 1, 1, s_b, m_b, s_a, m_a)
+    give7(0, 0)
+    pass_back(0)
     only_weigh(0, UNITS - 1, s_b, m_b)
     give7(0, 1)
-    pass_back(0)
     for load in loads[3:]:
         load.wait()
+    for side in range(2):
+        gather6(0, side)
     for h in range(2):
         causal(h)
-    for h in range(2):
-        gather6(0, h)
+    order = [(h, r) for r in range(2) for h in range(2)]
     for d in range(NEAR - 1, 0, -1):
-        for h in range(2):
-            back(0, d, h)
-    for h in range(2):
-        final(0, h)
+        for h, r in order:
+            back(0, d, h, r)
+    for h, r in order:
+        final(0, h, r)
 
     for side in range(2):
         for d in range(1, NEAR + 2):
@@ -483,11 +494,12 @@
     for w in range(WAVES):
         for side in range(2):
             for h in range(2):
-                for d in range(1, NEAR + 1):
-                    q_copy(w, side, d, h).wait_send()
-                    for copy in chain_copies(w, side, d, h):
-                        copy.wait_send()
-            for copy in [sel7_copy(w, side), sel8_copy(w, side), pass8_copy(w, side)]:
+                for r in range(2):
+                    for d in range(1, NEAR + 1):
+                        q_copy(w, side, d, h, r).wait_send()
+                        for copy in chain_copies(w, side, d, h, r):
+                            copy.wait_send()
+            for copy in [sel7_copy(w, side, r) for r in range(2)] + [sel8_copy(w, side), pass8_copy(w, side)]:
                 copy.wait_send()
             for copy in far8_copies(w, side) + far8_passes(w, side) + far7_copies(w, side):
                 copy.wait_send()
@@ -538,17 +550,17 @@
             pltpu.VMEM((WAVES, 2, blocks, LANES), F32),
             pltpu.VMEM((WAVES, 2, blocks, LANES, LANES), BF16),
             pltpu.VMEM((WAVES, 2, blocks, LANES), F32),
-            pltpu.VMEM((WAVES, 2, NEAR + 1, 2, blocks, LANES, LANES), BF16),
-            pltpu.VMEM((WAVES, 2, NEAR + 1, 2, blocks, LANES), F32),
+            pltpu.VMEM((WAVES, 2, NEAR + 1, 2, 2, half, LANES, LANES), BF16),
+            pltpu.VMEM((WAVES, 2, NEAR + 1, 2, 2, half, LANES), F32),
             pltpu.SemaphoreType.DMA((5,)),
-            pltpu.SemaphoreType.DMA((WAVES, 2, 8, 2)),
-            pltpu.SemaphoreType.DMA((WAVES, 2, 8, 2)),
+            pltpu.SemaphoreType.DMA((WAVES, 2, 8, 2, 2)),
+            pltpu.SemaphoreType.DMA((WAVES, 2, 8, 2, 2)),
             pltpu.SemaphoreType.DMA((2, 8)),
             pltpu.SemaphoreType.DMA((2, 8)),
             pltpu.SemaphoreType.DMA((WAVES, 2, 6)),
             pltpu.SemaphoreType.DMA((WAVES, 2, 6)),
-            pltpu.SemaphoreType.DMA((WAVES, 2, NEAR, 2, 2)),
-            pltpu.SemaphoreType.DMA((WAVES, 2, NEAR, 2, 2)),
+            pltpu.SemaphoreType.DMA((WAVES, 2, NEAR, 2, 2, 2)),
+            pltpu.SemaphoreType.DMA((WAVES, 2, NEAR, 2, 2, 2)),
         ],
         compiler_params=pltpu.CompilerParams(
             collective_id=0, has_side_effects=True, vmem_limit_bytes=56 * 1024 * 1024

time: 119 us -> 119 us (level)
  the two profiles are of different devices: /device:TPU:26 before, /device:TPU:2 now
where the time goes in v2:
time: 119 us
  Pallas kernels  117 us (98%)
  local copies, waits for them, and re-layouts  1.67 us (1%)
    pallas_call x1, Pallas kernels, shards(): pl.pallas_call(functools.partial(kernel, ranks, rate), out_shape=jax.Shap...  117 us

profile of v2, /device:TPU:2, one launch (start us, length us, event | category | flops | bytes accessed | tf_op | source)
XLA Modules:
  0.0 118.5 jit_solution(681453733574128129)
XLA Ops:
  0.0 116.9 %shard_map.64 = bf16[512,256]{1,0:T(8,128)(2,1)} custom-call(s32[1,2,3]{2,1,0:T(2,128)} %picks.1, bf16[512,256]{1,0:T(8,128)(2,1)} %q_in.1, bf16[512,256]{1,0:T(8,128)(2,1)} %ko_in.1, bf16[512,256]{1,0:T(8,128)(2,1)} %vo_in.1, bf16[4096,256]{1,0:T(8,128)(2,1)} %k_in.1, bf16[4096,256]{1,0:T(8,128)(2,1)} %v_in.1), custom_call_target="tpu_custom_call" | custom-call | flops 34359738368 | bytes 5242880 | tf_op jit(solution)/shard_map/pallas_call | solution.py:516
  116.9 1.7 %copy.8 = bf16[512,256]{1,0:T(8,128)(2,1)} copy(bf16[512,256]{1,0:T(8,128)(2,1)} %shard_map.64) | data formatting | bytes 524288

commit v3 on v2

--- a/solution.py
+++ b/solution.py
@@ -382,6 +382,7 @@
         for side in range(2):
             for copy in chain_copies(w, side, d + 1, h, r):
                 copy.wait_recv()
+        for side in range(2):
             u = slot(side, d)
             want = chosen(u, z)
             for k in range(half):
@@ -391,6 +392,7 @@
                 )
                 chain[w, side, d, h, r, k] = o.astype(BF16)
                 clse[w, side, d, h, r, k:k + 1, :] = lse
+        for side in range(2):
             for copy in chain_copies(w, side, d, h, r):
                 copy.start()
 

time: 119 us -> 119 us (level)
  the two profiles are of different devices: /device:TPU:2 before, /device:TPU:20 now
where the time goes in v3:
time: 119 us
  Pallas kernels  117 us (98%)
  local copies, waits for them, and re-layouts  1.67 us (1%)
    pallas_call x1, Pallas kernels, shards(): pl.pallas_call(functools.partial(kernel, ranks, rate), out_shape=jax.Shap...  117 us

profile of v3, /device:TPU:20, one launch (start us, length us, event | category | flops | bytes accessed | tf_op | source)
XLA Modules:
  0.0 118.6 jit_solution(11176937259156109836)
XLA Ops:
  0.0 116.9 %shard_map.64 = bf16[512,256]{1,0:T(8,128)(2,1)} custom-call(s32[1,2,3]{2,1,0:T(2,128)} %picks.1, bf16[512,256]{1,0:T(8,128)(2,1)} %q_in.1, bf16[512,256]{1,0:T(8,128)(2,1)} %ko_in.1, bf16[512,256]{1,0:T(8,128)(2,1)} %vo_in.1, bf16[4096,256]{1,0:T(8,128)(2,1)} %k_in.1, bf16[4096,256]{1,0:T(8,128)(2,1)} %v_in.1), custom_call_target="tpu_custom_call" | custom-call | flops 34359738368 | bytes 5242880 | tf_op jit(solution)/shard_map/pallas_call | solution.py:518
  116.9 1.7 %copy.8 = bf16[512,256]{1,0:T(8,128)(2,1)} copy(bf16[512,256]{1,0:T(8,128)(2,1)} %shard_map.64) | data formatting | bytes 524288
